TPU v7x, 512 devices: a whole 4x4x16 slice. The times are simulated.
512 devices in a mesh: face: 4 (over z_lo), tile: 64 (over y, z_hi, x), lev: 2 (over core).
Axes of the slice: x: 4, y: 4, z: 16 (z_hi: 4, z_lo: 4; z = z_hi * 4 + z_lo), core: 2. Of those that a mesh axis runs over, the one named last changes fastest.
Arguments:
- flux: float32 [2048, 8, 512], P(('face', 'tile')), may hold values from -6 to 6
- profile: float32 [16], P('lev'), may hold values from 0.2 to 1
- courant: float32 [2, 16, 512, 2048], P(None, 'lev', 'tile', 'face'), may hold values from 0.05 to 0.45
- winds: int32 [2, 16, 512, 2048], P(None, 'lev', 'tile', 'face'), may hold values from 0 to 1
- cells: int32 [64, 4, 128], P('tile', 'face'), may hold values from 0 to 4095, as said below
- counts: int32 [64, 4], P('tile', 'face'), may hold values from 32 to 128, as said below
- kernels: float32 [16, 64, 4, 128], P('lev', 'tile', 'face'), may hold values from 0.25 to 0.75
- month_weight: float32 [8, 64, 4, 128], P(None, 'tile', 'face'), may hold values from 0 to 1
- observed: float32 [64, 4, 128], P('tile', 'face'), may hold values from -8 to 8
- obs_weight: float32 [64, 4, 128], P('tile', 'face'), may hold values from 0.5 to 2
- precision: float32 [8], replicated, may hold values from 0.5 to 2
Outputs:
- flux_gradient: float32 [8, 512, 2048], P(None, 'tile', 'face')
- precision_gradient: float32 [8], replicated
Inputs may be any that keep to these rules, and one draw needn't show every extreme that they name: Within each block the 128 entries are distinct cells, numbered row by row over the block's 8 rows of 512 cells; the first four slots of every block hold, in some order, a cell of the block's first column, one of its last column, and interior cells of its first row and of its last row. `counts`: slot s of a block holds a sounding when s is below the block's count; some block is full and some holds exactly 32.
All inputs are finite; a program needn't handle non-finite values.
Results may differ from a plain program's by a relative error of at most 0.00015.
Values sent between devices are 32-bit elements; how exact they have to be, the bound alone decides.
A program may use at most 64 MiB of HBM per device.

v0:
```python
import jax
import jax.numpy as jnp
from jax import lax
from jax.sharding import PartitionSpec as P

KAPPA = 0.025


def extended(x, sides, width, wrap):
    for axis, dim in sides:
        devices, length = (lax.axis_size(axis), x.shape[dim])
        up = [(i, (i + 1) % devices) for i in range(devices if wrap else devices - 1)]
        down = [(j, i) for i, j in up]
        last = lax.slice_in_dim(x, length - width, length, axis=dim)
        initial = lax.slice_in_dim(x, 0, width, axis=dim)
        before = lax.ppermute(last, axis, up)
        after = lax.ppermute(initial, axis, down)
        x = jnp.concatenate([before, x, after], axis=dim)
    return x


def shifted(x, axis, by):
    devices = lax.axis_size(axis)
    return lax.ppermute(x, axis, [(i, (i + by) % devices) for i in range(devices)])


def shifted_2(value, axis, steps):
    count = lax.axis_size(axis)
    initial, last = (max(0, -steps), min(count, count - steps))
    return lax.ppermute(value, axis, [(source, source + steps) for source in range(initial, last)])


def weights_from(speed_x, speed_y, east_flag, north_flag):
    w_west = speed_x * (1.0 - east_flag) + KAPPA
    w_east = speed_x * east_flag + KAPPA
    w_south = speed_y * (1.0 - north_flag) + KAPPA
    w_north = speed_y * north_flag + KAPPA
    w_centre = 1.0 - speed_x - speed_y - 4.0 * KAPPA
    return (w_centre, w_west, w_east, w_south, w_north)


def flags_of(winds):
    return ((winds[0] == 1).astype(jnp.float32), (winds[1] == 1).astype(jnp.float32))


def advance(conc, coeffs):
    w_centre, w_west, w_east, w_south, w_north = coeffs
    side = extended(conc, (("face", 3),), 1, True)
    rim = extended(conc, (("tile", 2),), 1, False)
    return (
        w_centre * conc
        + w_west * side[..., :-2]
        + w_east * side[..., 2:]
        + w_south * rim[..., :-2, :]
        + w_north * rim[..., 2:, :]
    )


def retreat(grad, coeffs):
    w_centre, w_west, w_east, w_south, w_north = coeffs
    west_weighted = w_west * grad
    east_weighted = w_east * grad
    south_weighted = w_south * grad
    north_weighted = w_north * grad
    from_east = shifted(west_weighted[..., :1], "face", -1)
    from_west = shifted(east_weighted[..., -1:], "face", 1)
    from_above = shifted_2(south_weighted[..., :1, :], "tile", -1)
    from_below = shifted_2(north_weighted[..., -1:, :], "tile", 1)
    west_part = jnp.concatenate([west_weighted[..., 1:], from_east], -1)
    east_part = jnp.concatenate([from_west, east_weighted[..., :-1]], -1)
    south_part = jnp.concatenate([south_weighted[..., 1:, :], from_above], -2)
    north_part = jnp.concatenate([from_below, north_weighted[..., :-1, :]], -2)
    return w_centre * grad + west_part + east_part + south_part + north_part


def on_device(
    flux,
    profile,
    courant,
    winds,
    cells,
    counts,
    kernels,
    month_weight,
    observed,
    obs_weight,
    precision,
):
    n_tracer = flux.shape[1]
    n_level = profile.shape[0]
    slot_total = cells.shape[2]
    moved = lax.all_to_all(flux, "tile", split_axis=2, concat_axis=0, tiled=True)
    field = jnp.transpose(moved, (1, 2, 0))
    rows_dev = field.shape[1]
    cols_dev = field.shape[2]
    n_cell = rows_dev * cols_dev
    east_flag, north_flag = flags_of(winds)
    conc = profile[None, :, None, None] * field[:, None]
    coeffs = weights_from(courant[0], courant[1], east_flag, north_flag)
    conc = advance(advance(conc, coeffs), coeffs)
    slot_cells = cells.reshape(slot_total)
    live = jnp.arange(slot_total, dtype=jnp.int32) < counts.reshape(())
    picker = jnp.where(
        live[:, None] & (slot_cells[:, None] == jnp.arange(n_cell, dtype=jnp.int32)[None, :]),
        1.0,
        0.0,
    ).astype(jnp.float32)
    flat = conc.reshape(n_tracer, n_level, n_cell)
    sampled = jnp.einsum("tlc,sc->tls", flat, picker, precision=lax.Precision.HIGHEST)
    kern = kernels.reshape(n_level, slot_total)
    monthly = month_weight.reshape(n_tracer, slot_total)
    partial_model = jnp.sum(kern * jnp.sum(monthly[:, None, :] * sampled, 0), 0)
    model = lax.psum(partial_model, "lev")
    forcing = jnp.where(
        live, obs_weight.reshape(slot_total) * (observed.reshape(slot_total) - model), 0.0
    )
    values = kern[None] * (monthly * forcing[None])[:, None, :]
    lam = jnp.einsum("tls,sc->tlc", values, picker, precision=lax.Precision.HIGHEST)
    lam = lam.reshape(n_tracer, n_level, rows_dev, cols_dev)
    lam = retreat(retreat(lam, coeffs), coeffs)
    adj_part = jnp.sum(profile[None, :, None, None] * lam, 1)
    all_cells = n_cell * lax.axis_size("tile") * lax.axis_size("face")
    adj = lax.psum(adj_part, "lev")
    flux_gradient = precision[:, None, None] * field - adj
    square_sum = lax.psum(jnp.sum(adj * adj, axis=(1, 2)), ("face", "tile"))
    precision_gradient = 0.5 / precision - 0.5 * (square_sum / all_cells) / (precision * precision)
    return (flux_gradient, precision_gradient)


def solution(mesh):
    return jax.shard_map(
        on_device,
        mesh=mesh,
        in_specs=(
            P(("face", "tile"), None, None),
            P("lev"),
            P(None, "lev", "tile", "face"),
            P(None, "lev", "tile", "face"),
            P("tile", "face", None),
            P("tile", "face"),
            P("lev", "tile", "face", None),
            P(None, "tile", "face", None),
            P("tile", "face", None),
            P("tile", "face", None),
            P(),
        ),
        out_specs=(P(None, "tile", "face"), P()),
        check_vma=False,
    )
```

profile of v0, /device:TPU:32, one launch (start us, length us, event | category | flops | bytes accessed | tf_op | source)
XLA Modules:
  0.0 1168.7 jit_solution(5610475102505204907)
XLA Ops:
  7.2 1.7 copy.25
  8.9 1.7 reshape.69
  10.6 20.3 %all-to-all-start = ((f32[64,1,512]{2,1,0:T(1,128)}), f32[64,1,512]{2,1,0:T(1,128)S(1)}, u32[]{:S(2)}, u32[]{:S(2)}) async-start(f32[64,1,512]{2,1,0:T(1,128)} %reshape.69), calls=%async_computation | async-start | bytes 262144 | tf_op jit(solution)/shard_map/all_to_all | solution.py:92
  31.1 20.0 %all-to-all-done = f32[64,1,512]{2,1,0:T(1,128)S(1)} async-done(((f32[64,1,512]{2,1,0:T(1,128)}), f32[64,1,512]{2,1,0:T(1,128)S(1)}, u32[]{:S(2)}, u32[]{:S(2)}) %all-to-all-start) | async-done | bytes 131104 | tf_op jit(solution)/shard_map/all_to_all | solution.py:92
  53.7 2.4 copy.27
  56.1 2.8 all_to_all.16
  59.3 2.5 collective-permute-start.2
  61.8 1.3 collective-permute-start.3
  63.1 2.9 collective-permute-start
  66.1 2.9 collective-permute-start.1
  70.1 4.1 collective-permute-done
  74.2 7.7 collective-permute-done.1
  82.7 1.3 collective-permute-start.6
  85.5 5.5 collective-permute-start.4
  91.0 1.9 collective-permute-start.5
  93.0 7.6 collective-permute-done.4
  101.3 2.4 fusion.12
  103.8 2.6 psum.21
  106.5 1.7 fusion
  110.1 4.9 collective-permute-start.11
  115.2 3.2 collective-permute-start.8
  118.4 3.1 collective-permute-start.9
  122.2 3.8 collective-permute-done.8
  126.0 6.6 collective-permute-done.9
  133.6 4.2 collective-permute-start.12
  138.6 5.9 collective-permute-start.15
  146.0 3.7 collective-permute-start.13
  149.8 7.5 collective-permute-done.13
  157.8 9.1 collective-permute-done.14
  168.8 66.5 %all-reduce.2.cloned.1.call-done = f32[8,8,512]{2,1,0:T(8,128)} async-done(((f32[8,8,512]{2,1,0:T(8,128)}), f32[8,8,512]{2,1,0:T(8,128)}) %all-reduce.2.cloned.1.call-update) | async-done | bytes 131088 | tf_op jit(solution)/shard_map/psum | solution.py:123
  235.3 1.7 multiply_reduce_fusion.1
  237.0 924.4 %psum.23 = f32[8]{0:T(128)S(1)} all-reduce(f32[8]{0:T(128)S(1)} %get-tuple-element.33), channel_id=1, replica_groups=mesh['face'=4,'tile'=64,'lev'=2] {'face','tile'}, use_global_device_ids=true, to_apply=%region_6.7 | all-reduce | flops 8 | bytes 64 | tf_op jit(solution)/shard_map/psum | solution.py:125
  (78 shorter events, 15.5 us)
Async XLA Ops:
  7.2 23.8 %copy-start = (f32[2,8,8,512]{3,2,1,0:T(8,128)S(1)}, f32[2,8,8,512]{3,2,1,0:T(8,128)}, u32[]{:S(2)}) copy-start(f32[2,8,8,512]{3,2,1,0:T(8,128)} %param.13) | copy-start | bytes 786436
  7.2 23.8 %copy-start.1 = (s32[2,8,8,512]{3,2,1,0:T(8,128)S(1)}, s32[2,8,8,512]{3,2,1,0:T(8,128)}, u32[]{:S(2)}) copy-start(s32[2,8,8,512]{3,2,1,0:T(8,128)} %param.14) | copy-start | bytes 786436
  10.6 40.5 %all-to-all-start = ((f32[64,1,512]{2,1,0:T(1,128)}), f32[64,1,512]{2,1,0:T(1,128)S(1)}, u32[]{:S(2)}, u32[]{:S(2)}) async-start(f32[64,1,512]{2,1,0:T(1,128)} %reshape.69), calls=%async_computation | async-start | bytes 262144 | tf_op jit(solution)/shard_map/all_to_all | solution.py:92
  30.9 204.3 %all-reduce.2.cloned.1.call-start = ((), (), s32[]{:S(2)}) async-start(), calls=%async_computation.1 | async-start | bytes 262144 | tf_op jit(solution)/shard_map/psum | solution.py:123
  56.1 2.8 copy-start.4
  59.3 22.6 %collective-permute-start.2 = (f32[8,8,1,512]{3,1,2,0:T(8,128)S(1)}, f32[8,8,1,512]{3,1,2,0:T(8,128)S(1)}, u32[]{:S(2)}, u32[]{:S(2)}) collective-permute-start(f32[8,8,1,512]{3,1,2,0:T(8,128)S(1)} %get-tuple-element.25), channel_id=1, source_target_pairs={{0,2},{2,4},{4,6},{6,8},{8,10},{10,12},{12,14},{14,16},{16,18},{18... | collective-permute-start | bytes 393224 | tf_op jit(solution)/shard_map/ppermute | solution.py:16
  61.8 20.1 %collective-permute-start.3 = (f32[8,8,1,512]{3,1,2,0:T(8,128)S(1)}, f32[8,8,1,512]{3,1,2,0:T(8,128)S(1)}, u32[]{:S(2)}, u32[]{:S(2)}) collective-permute-start(f32[8,8,1,512]{3,1,2,0:T(8,128)S(1)} %get-tuple-element.26), channel_id=1, source_target_pairs={{2,0},{4,2},{6,4},{8,6},{10,8},{12,10},{14,12},{16,14},{18,16},{20... | collective-permute-start | bytes 393224 | tf_op jit(solution)/shard_map/ppermute | solution.py:17
  63.1 11.1 collective-permute-start
  66.1 15.9 %collective-permute-start.1 = (f32[8,8,8,1]{3,1,2,0:T(8,128)S(1)}, f32[8,8,8,1]{3,1,2,0:T(8,128)S(1)}, u32[]{:S(2)}, u32[]{:S(2)}) collective-permute-start(f32[8,8,8,1]{3,1,2,0:T(8,128)S(1)} %get-tuple-element.24), channel_id=1, source_target_pairs={{128,0},{256,128},{384,256},{0,384},{129,1},{257,129},{385,257},{1... | collective-permute-start | bytes 6152 | tf_op jit(solution)/shard_map/ppermute | solution.py:17
  82.7 17.8 %collective-permute-start.6 = (f32[8,8,1,512]{3,1,2,0:T(8,128)S(1)}, f32[8,8,1,512]{3,1,2,0:T(8,128)S(1)}, u32[]{:S(2)}, u32[]{:S(2)}) collective-permute-start(f32[8,8,1,512]{3,1,2,0:T(8,128)S(1)} %get-tuple-element.21), channel_id=1, source_target_pairs={{0,2},{2,4},{4,6},{6,8},{8,10},{10,12},{12,14},{14,16},{16,18},{18... | collective-permute-start | bytes 393224 | tf_op jit(solution)/shard_map/ppermute | solution.py:16
  84.0 17.3 %copy-start.2 = (f32[8,1,1,128]{3,2,1,0:T(1,128)S(1)}, f32[8,1,1,128]{3,2,1,0:T(1,128)}, u32[]{:S(2)}) copy-start(f32[8,1,1,128]{3,2,1,0:T(1,128)} %param.18) | copy-start | bytes 12292
  84.0 17.3 %copy-start.8 = (s32[1,1,128]{2,1,0:T(1,128)S(1)}, s32[1,1,128]{2,1,0:T(1,128)}, u32[]{:S(2)}) copy-start(s32[1,1,128]{2,1,0:T(1,128)} %param.15) | copy-start | bytes 1540
  84.0 16.5 %collective-permute-start.7 = (f32[8,8,1,512]{3,1,2,0:T(8,128)S(1)}, f32[8,8,1,512]{3,1,2,0:T(8,128)S(1)}, u32[]{:S(2)}, u32[]{:S(2)}) collective-permute-start(f32[8,8,1,512]{3,1,2,0:T(8,128)S(1)} %get-tuple-element.22), channel_id=1, source_target_pairs={{2,0},{4,2},{6,4},{8,6},{10,8},{12,10},{14,12},{16,14},{18,16},{20... | collective-permute-start | bytes 393224 | tf_op jit(solution)/shard_map/ppermute | solution.py:17
  85.5 15.0 %collective-permute-start.4 = (f32[8,8,8,1]{3,1,2,0:T(8,128)S(1)}, f32[8,8,8,1]{3,1,2,0:T(8,128)S(1)}, u32[]{:S(2)}, u32[]{:S(2)}) collective-permute-start(f32[8,8,8,1]{3,1,2,0:T(8,128)S(1)} %get-tuple-element.19), channel_id=1, source_target_pairs={{0,128},{128,256},{256,384},{384,0},{1,129},{129,257},{257,385},{3... | collective-permute-start | bytes 6152 | tf_op jit(solution)/shard_map/ppermute | solution.py:16
  91.0 9.6 collective-permute-start.5
  92.9 10.9 copy-start.3
  92.9 13.5 %copy-start.6 = (f32[1,1,128]{2,1,0:T(1,128)S(1)}, f32[1,1,128]{2,1,0:T(1,128)}, u32[]{:S(2)}) copy-start(f32[1,1,128]{2,1,0:T(1,128)} %param.19) | copy-start | bytes 1540
  92.9 13.5 %copy-start.7 = (f32[1,1,128]{2,1,0:T(1,128)S(1)}, f32[1,1,128]{2,1,0:T(1,128)}, u32[]{:S(2)}) copy-start(f32[1,1,128]{2,1,0:T(1,128)} %param.20) | copy-start | bytes 1540
  108.8 23.7 %collective-permute-start.10 = (f32[8,8,1,512]{3,1,2,0:T(8,128)S(1)}, f32[8,8,1,512]{3,1,2,0:T(8,128)S(1)}, u32[]{:S(2)}, u32[]{:S(2)}) collective-permute-start(f32[8,8,1,512]{3,1,2,0:T(8,128)S(1)} %slice.165), channel_id=1, source_target_pairs={{2,0},{4,2},{6,4},{8,6},{10,8},{12,10},{14,12},{16,14},{18,16},{20... | collective-permute-start | bytes 393224 | tf_op jit(solution)/shard_map/ppermute | solution.py:30
  110.1 22.4 %collective-permute-start.11 = (f32[8,8,1,512]{3,1,2,0:T(8,128)S(1)}, f32[8,8,1,512]{3,1,2,0:T(8,128)S(1)}, u32[]{:S(2)}, u32[]{:S(2)}) collective-permute-start(f32[8,8,1,512]{3,1,2,0:T(8,128)S(1)} %slice.166), channel_id=1, source_target_pairs={{0,2},{2,4},{4,6},{6,8},{8,10},{10,12},{12,14},{14,16},{16,18},{18... | collective-permute-start | bytes 393224 | tf_op jit(solution)/shard_map/ppermute | solution.py:30
  115.2 10.7 collective-permute-start.8
  118.4 14.1 %collective-permute-start.9 = (f32[8,8,8,1]{3,1,2,0:T(8,128)S(1)}, f32[8,8,8,1]{3,1,2,0:T(8,128)S(1)}, u32[]{:S(2)}, u32[]{:S(2)}) collective-permute-start(f32[8,8,8,1]{3,1,2,0:T(8,128)S(1)} %slice.162), channel_id=1, source_target_pairs={{0,128},{128,256},{256,384},{384,0},{1,129},{129,257},{257,385},{3... | collective-permute-start | bytes 6152 | tf_op jit(solution)/shard_map/ppermute | solution.py:24
  133.6 16.0 %collective-permute-start.12 = (f32[8,8,8,1]{3,1,2,0:T(8,128)S(1)}, f32[8,8,8,1]{3,1,2,0:T(8,128)S(1)}, u32[]{:S(2)}, u32[]{:S(2)}) collective-permute-start(f32[8,8,8,1]{3,1,2,0:T(8,128)S(1)} %slice.169), channel_id=1, source_target_pairs={{0,384},{128,0},{256,128},{384,256},{1,385},{129,1},{257,129},{385... | collective-permute-start | bytes 6152 | tf_op jit(solution)/shard_map/ppermute | solution.py:24
  138.6 19.1 %collective-permute-start.15 = (f32[8,8,1,512]{3,1,2,0:T(8,128)S(1)}, f32[8,8,1,512]{3,1,2,0:T(8,128)S(1)}, u32[]{:S(2)}, u32[]{:S(2)}) collective-permute-start(f32[8,8,1,512]{3,1,2,0:T(8,128)S(1)} %slice.174), channel_id=1, source_target_pairs={{0,2},{2,4},{4,6},{6,8},{8,10},{10,12},{12,14},{14,16},{16,18},{18... | collective-permute-start | bytes 393224 | tf_op jit(solution)/shard_map/ppermute | solution.py:30
  144.5 22.3 %collective-permute-start.14 = (f32[8,8,1,512]{3,1,2,0:T(8,128)S(1)}, f32[8,8,1,512]{3,1,2,0:T(8,128)S(1)}, u32[]{:S(2)}, u32[]{:S(2)}) collective-permute-start(f32[8,8,1,512]{3,1,2,0:T(8,128)S(1)} %slice.173), channel_id=1, source_target_pairs={{2,0},{4,2},{6,4},{8,6},{10,8},{12,10},{14,12},{16,14},{18,16},{20... | collective-permute-start | bytes 393224 | tf_op jit(solution)/shard_map/ppermute | solution.py:30
  146.0 11.4 collective-permute-start.13
  166.9 68.3 %copy-start.5 = (f32[8]{0:T(128)S(1)}, f32[8]{0:T(128)}, u32[]{:S(2)}) copy-start(f32[8]{0:T(128)} %param.21) | copy-start | bytes 100
Sparse Core Ops, SparseCore 0:
  169.0 66.2 all-reduce.1
where the time goes:
time: 1170 us
  blocking collectives  927 us (79%)
  waiting for transfers between devices  133 us (11%)
  starting transfers between devices  67.6 us (6%)
  between operations  15.2 us (1%)
  local copies, waits for them, and re-layouts  13.2 us (1%)
    psum x1, blocking collectives, on_device(): square_sum = lax.psum(jnp.sum(adj * adj, axis=(1, 2)), ('face', 'tile'))  924 us
    psum x1, waiting for transfers between devices, on_device(): adj = lax.psum(adj_part, 'lev')  66.5 us
  transfers between devices with their start and end apart: 18, of which 9 were waited for; matrix products, arithmetic and copies ran while one was open for 0% of the time, Pallas kernels for 0%

commit v1 on v0

--- a/solution.py
+++ b/solution.py
@@ -120,7 +120,7 @@
     lam = retreat(retreat(lam, coeffs), coeffs)
     adj_part = jnp.sum(profile[None, :, None, None] * lam, 1)
     all_cells = n_cell * lax.axis_size("tile") * lax.axis_size("face")
-    adj = lax.psum(adj_part, "lev")
+    adj = jnp.sum(lax.all_gather(adj_part, "lev"), axis=0)
     flux_gradient = precision[:, None, None] * field - adj
     square_sum = lax.psum(jnp.sum(adj * adj, axis=(1, 2)), ("face", "tile"))
     precision_gradient = 0.5 / precision - 0.5 * (square_sum / all_cells) / (precision * precision)

time: 1170 us -> 1100 us (0.940)
  the two profiles are of different devices: /device:TPU:32 before, /device:TPU:64 now
where the time goes in v1:
time: 1100 us
  blocking collectives  945 us (86%)
  waiting for transfers between devices  65.2 us (6%)
  starting transfers between devices  64.7 us (6%)
  local copies, waits for them, and re-layouts  12.6 us (1%)
    psum x1, blocking collectives, on_device(): square_sum = lax.psum(jnp.sum(adj * adj, axis=(1, 2)), ('face', 'tile'))  941 us
  transfers between devices with their start and end apart: 17, of which 9 were waited for; matrix products, arithmetic and copies ran while one was open for 0% of the time, Pallas kernels for 0%

profile of v1, /device:TPU:64, one launch (start us, length us, event | category | flops | bytes accessed | tf_op | source)
XLA Modules:
  0.0 1101.2 jit_solution(3678466900896953638)
XLA Ops:
  0.6 1.7 copy.25
  2.4 1.7 reshape.70
  4.1 19.4 %all-to-all-start = ((f32[64,1,512]{2,1,0:T(1,128)}), f32[64,1,512]{2,1,0:T(1,128)S(1)}, u32[]{:S(2)}, u32[]{:S(2)}) async-start(f32[64,1,512]{2,1,0:T(1,128)} %reshape.70), calls=%async_computation | async-start | bytes 262144 | tf_op jit(solution)/shard_map/all_to_all | solution.py:92
  23.6 20.1 %all-to-all-done = f32[64,1,512]{2,1,0:T(1,128)S(1)} async-done(((f32[64,1,512]{2,1,0:T(1,128)}), f32[64,1,512]{2,1,0:T(1,128)S(1)}, u32[]{:S(2)}, u32[]{:S(2)}) %all-to-all-start) | async-done | bytes 131104 | tf_op jit(solution)/shard_map/all_to_all | solution.py:92
  46.3 2.4 copy.27
  48.7 2.8 all_to_all.16
  51.8 2.5 collective-permute-start.2
  54.4 1.3 collective-permute-start.3
  55.7 1.9 collective-permute-start
  57.6 3.9 collective-permute-start.1
  62.7 3.6 collective-permute-done
  66.3 10.7 collective-permute-done.1
  77.8 1.3 collective-permute-start.6
  80.6 1.9 collective-permute-start.4
  82.5 3.9 collective-permute-start.5
  86.5 8.0 collective-permute-done.4
  95.3 2.4 fusion.12
  97.8 2.6 psum.14
  100.5 1.7 fusion
  103.9 4.9 collective-permute-start.11
  109.0 1.9 collective-permute-start.8
  110.9 3.9 collective-permute-start.9
  115.4 4.9 collective-permute-done.8
  120.3 4.9 collective-permute-done.9
  126.3 2.5 collective-permute-start.12
  129.7 8.0 collective-permute-start.15
  139.1 3.3 collective-permute-start.13
  142.5 2.4 collective-permute-done.12
  145.0 3.4 collective-permute-done.13
  148.8 7.2 collective-permute-done.14
  157.4 2.0 all_gather.7
  160.2 940.6 %psum.15 = f32[8]{0:T(128)S(1)} all-reduce(f32[8]{0:T(128)S(1)} %get-tuple-element.33), channel_id=1, replica_groups=mesh['face'=4,'tile'=64,'lev'=2] {'face','tile'}, use_global_device_ids=true, to_apply=%region_6.7 | all-reduce | flops 8 | bytes 64 | tf_op jit(solution)/shard_map/psum | solution.py:125
  (77 shorter events, 15.4 us)
Async XLA Ops:
  0.6 22.9 %copy-start = (f32[2,8,8,512]{3,2,1,0:T(8,128)S(1)}, f32[2,8,8,512]{3,2,1,0:T(8,128)}, u32[]{:S(2)}) copy-start(f32[2,8,8,512]{3,2,1,0:T(8,128)} %param.13) | copy-start | bytes 786436
  0.6 22.9 %copy-start.1 = (s32[2,8,8,512]{3,2,1,0:T(8,128)S(1)}, s32[2,8,8,512]{3,2,1,0:T(8,128)}, u32[]{:S(2)}) copy-start(s32[2,8,8,512]{3,2,1,0:T(8,128)} %param.14) | copy-start | bytes 786436
  4.1 39.6 %all-to-all-start = ((f32[64,1,512]{2,1,0:T(1,128)}), f32[64,1,512]{2,1,0:T(1,128)S(1)}, u32[]{:S(2)}, u32[]{:S(2)}) async-start(f32[64,1,512]{2,1,0:T(1,128)} %reshape.70), calls=%async_computation | async-start | bytes 262144 | tf_op jit(solution)/shard_map/all_to_all | solution.py:92
  48.7 2.8 copy-start.4
  51.8 25.2 %collective-permute-start.2 = (f32[8,8,1,512]{3,1,2,0:T(8,128)S(1)}, f32[8,8,1,512]{3,1,2,0:T(8,128)S(1)}, u32[]{:S(2)}, u32[]{:S(2)}) collective-permute-start(f32[8,8,1,512]{3,1,2,0:T(8,128)S(1)} %get-tuple-element.25), channel_id=1, source_target_pairs={{0,2},{2,4},{4,6},{6,8},{8,10},{10,12},{12,14},{14,16},{16,18},{18... | collective-permute-start | bytes 393224 | tf_op jit(solution)/shard_map/ppermute | solution.py:16
  54.4 22.7 %collective-permute-start.3 = (f32[8,8,1,512]{3,1,2,0:T(8,128)S(1)}, f32[8,8,1,512]{3,1,2,0:T(8,128)S(1)}, u32[]{:S(2)}, u32[]{:S(2)}) collective-permute-start(f32[8,8,1,512]{3,1,2,0:T(8,128)S(1)} %get-tuple-element.26), channel_id=1, source_target_pairs={{2,0},{4,2},{6,4},{8,6},{10,8},{12,10},{14,12},{16,14},{18,16},{20... | collective-permute-start | bytes 393224 | tf_op jit(solution)/shard_map/ppermute | solution.py:17
  55.7 10.6 collective-permute-start
  57.6 19.4 %collective-permute-start.1 = (f32[8,8,8,1]{3,1,2,0:T(8,128)S(1)}, f32[8,8,8,1]{3,1,2,0:T(8,128)S(1)}, u32[]{:S(2)}, u32[]{:S(2)}) collective-permute-start(f32[8,8,8,1]{3,1,2,0:T(8,128)S(1)} %get-tuple-element.24), channel_id=1, source_target_pairs={{128,0},{256,128},{384,256},{0,384},{129,1},{257,129},{385,257},{1... | collective-permute-start | bytes 6152 | tf_op jit(solution)/shard_map/ppermute | solution.py:17
  77.8 16.7 %collective-permute-start.6 = (f32[8,8,1,512]{3,1,2,0:T(8,128)S(1)}, f32[8,8,1,512]{3,1,2,0:T(8,128)S(1)}, u32[]{:S(2)}, u32[]{:S(2)}) collective-permute-start(f32[8,8,1,512]{3,1,2,0:T(8,128)S(1)} %get-tuple-element.21), channel_id=1, source_target_pairs={{0,2},{2,4},{4,6},{6,8},{8,10},{10,12},{12,14},{14,16},{16,18},{18... | collective-permute-start | bytes 393224 | tf_op jit(solution)/shard_map/ppermute | solution.py:16
  79.1 16.2 %copy-start.2 = (f32[8,1,1,128]{3,2,1,0:T(1,128)S(1)}, f32[8,1,1,128]{3,2,1,0:T(1,128)}, u32[]{:S(2)}) copy-start(f32[8,1,1,128]{3,2,1,0:T(1,128)} %param.18) | copy-start | bytes 12292
  79.2 16.2 %copy-start.8 = (s32[1,1,128]{2,1,0:T(1,128)S(1)}, s32[1,1,128]{2,1,0:T(1,128)}, u32[]{:S(2)}) copy-start(s32[1,1,128]{2,1,0:T(1,128)} %param.15) | copy-start | bytes 1540
  79.2 15.4 %collective-permute-start.7 = (f32[8,8,1,512]{3,1,2,0:T(8,128)S(1)}, f32[8,8,1,512]{3,1,2,0:T(8,128)S(1)}, u32[]{:S(2)}, u32[]{:S(2)}) collective-permute-start(f32[8,8,1,512]{3,1,2,0:T(8,128)S(1)} %get-tuple-element.22), channel_id=1, source_target_pairs={{2,0},{4,2},{6,4},{8,6},{10,8},{12,10},{14,12},{16,14},{18,16},{20... | collective-permute-start | bytes 393224 | tf_op jit(solution)/shard_map/ppermute | solution.py:17
  80.6 14.0 %collective-permute-start.4 = (f32[8,8,8,1]{3,1,2,0:T(8,128)S(1)}, f32[8,8,8,1]{3,1,2,0:T(8,128)S(1)}, u32[]{:S(2)}, u32[]{:S(2)}) collective-permute-start(f32[8,8,8,1]{3,1,2,0:T(8,128)S(1)} %get-tuple-element.19), channel_id=1, source_target_pairs={{0,128},{128,256},{256,384},{384,0},{1,129},{129,257},{257,385},{3... | collective-permute-start | bytes 6152 | tf_op jit(solution)/shard_map/ppermute | solution.py:16
  82.5 12.0 %collective-permute-start.5 = (f32[8,8,8,1]{3,1,2,0:T(8,128)S(1)}, f32[8,8,8,1]{3,1,2,0:T(8,128)S(1)}, u32[]{:S(2)}, u32[]{:S(2)}) collective-permute-start(f32[8,8,8,1]{3,1,2,0:T(8,128)S(1)} %get-tuple-element.20), channel_id=1, source_target_pairs={{128,0},{256,128},{384,256},{0,384},{129,1},{257,129},{385,257},{1... | collective-permute-start | bytes 6152 | tf_op jit(solution)/shard_map/ppermute | solution.py:17
  86.5 11.3 %copy-start.3 = (f32[8,1,1,128]{3,2,1,0:T(1,128)S(1)}, f32[8,1,1,128]{3,2,1,0:T(1,128)}, u32[]{:S(2)}) copy-start(f32[8,1,1,128]{3,2,1,0:T(1,128)} %param.17) | copy-start | bytes 12292
  86.5 14.0 %copy-start.6 = (f32[1,1,128]{2,1,0:T(1,128)S(1)}, f32[1,1,128]{2,1,0:T(1,128)}, u32[]{:S(2)}) copy-start(f32[1,1,128]{2,1,0:T(1,128)} %param.19) | copy-start | bytes 1540
  86.5 14.0 %copy-start.7 = (f32[1,1,128]{2,1,0:T(1,128)S(1)}, f32[1,1,128]{2,1,0:T(1,128)}, u32[]{:S(2)}) copy-start(f32[1,1,128]{2,1,0:T(1,128)} %param.20) | copy-start | bytes 1540
  102.6 22.6 %collective-permute-start.10 = (f32[8,8,1,512]{3,1,2,0:T(8,128)S(1)}, f32[8,8,1,512]{3,1,2,0:T(8,128)S(1)}, u32[]{:S(2)}, u32[]{:S(2)}) collective-permute-start(f32[8,8,1,512]{3,1,2,0:T(8,128)S(1)} %slice.165), channel_id=1, source_target_pairs={{2,0},{4,2},{6,4},{8,6},{10,8},{12,10},{14,12},{16,14},{18,16},{20... | collective-permute-start | bytes 393224 | tf_op jit(solution)/shard_map/ppermute | solution.py:30
  103.9 21.3 %collective-permute-start.11 = (f32[8,8,1,512]{3,1,2,0:T(8,128)S(1)}, f32[8,8,1,512]{3,1,2,0:T(8,128)S(1)}, u32[]{:S(2)}, u32[]{:S(2)}) collective-permute-start(f32[8,8,1,512]{3,1,2,0:T(8,128)S(1)} %slice.166), channel_id=1, source_target_pairs={{0,2},{2,4},{4,6},{6,8},{8,10},{10,12},{12,14},{14,16},{16,18},{18... | collective-permute-start | bytes 393224 | tf_op jit(solution)/shard_map/ppermute | solution.py:30
  109.0 11.3 %collective-permute-start.8 = (f32[8,8,8,1]{3,1,2,0:T(8,128)S(1)}, f32[8,8,8,1]{3,1,2,0:T(8,128)S(1)}, u32[]{:S(2)}, u32[]{:S(2)}) collective-permute-start(f32[8,8,8,1]{3,1,2,0:T(8,128)S(1)} %slice.161), channel_id=1, source_target_pairs={{0,384},{128,0},{256,128},{384,256},{1,385},{129,1},{257,129},{385... | collective-permute-start | bytes 6152 | tf_op jit(solution)/shard_map/ppermute | solution.py:24
  110.9 14.3 %collective-permute-start.9 = (f32[8,8,8,1]{3,1,2,0:T(8,128)S(1)}, f32[8,8,8,1]{3,1,2,0:T(8,128)S(1)}, u32[]{:S(2)}, u32[]{:S(2)}) collective-permute-start(f32[8,8,8,1]{3,1,2,0:T(8,128)S(1)} %slice.162), channel_id=1, source_target_pairs={{0,128},{128,256},{256,384},{384,0},{1,129},{129,257},{257,385},{3... | collective-permute-start | bytes 6152 | tf_op jit(solution)/shard_map/ppermute | solution.py:24
  126.3 18.5 %collective-permute-start.12 = (f32[8,8,8,1]{3,1,2,0:T(8,128)S(1)}, f32[8,8,8,1]{3,1,2,0:T(8,128)S(1)}, u32[]{:S(2)}, u32[]{:S(2)}) collective-permute-start(f32[8,8,8,1]{3,1,2,0:T(8,128)S(1)} %slice.169), channel_id=1, source_target_pairs={{0,384},{128,0},{256,128},{384,256},{1,385},{129,1},{257,129},{385... | collective-permute-start | bytes 6152 | tf_op jit(solution)/shard_map/ppermute | solution.py:24
  129.7 19.0 %collective-permute-start.15 = (f32[8,8,1,512]{3,1,2,0:T(8,128)S(1)}, f32[8,8,1,512]{3,1,2,0:T(8,128)S(1)}, u32[]{:S(2)}, u32[]{:S(2)}) collective-permute-start(f32[8,8,1,512]{3,1,2,0:T(8,128)S(1)} %slice.174), channel_id=1, source_target_pairs={{0,2},{2,4},{4,6},{6,8},{8,10},{10,12},{12,14},{14,16},{16,18},{18... | collective-permute-start | bytes 393224 | tf_op jit(solution)/shard_map/ppermute | solution.py:30
  137.7 18.3 %collective-permute-start.14 = (f32[8,8,1,512]{3,1,2,0:T(8,128)S(1)}, f32[8,8,1,512]{3,1,2,0:T(8,128)S(1)}, u32[]{:S(2)}, u32[]{:S(2)}) collective-permute-start(f32[8,8,1,512]{3,1,2,0:T(8,128)S(1)} %slice.173), channel_id=1, source_target_pairs={{2,0},{4,2},{6,4},{8,6},{10,8},{12,10},{14,12},{16,14},{18,16},{20... | collective-permute-start | bytes 393224 | tf_op jit(solution)/shard_map/ppermute | solution.py:30
  139.1 9.2 collective-permute-start.13
  156.1 3.2 copy-start.5
